TPU v7x, 32 devices: a whole 2x2x4 slice. The times are simulated.
32 devices in a mesh: orb: 8 (over z, core), aux: 4 (over y, x).
Axes of the slice: x: 2, y: 2, z: 4, core: 2. Of those that a mesh axis runs over, the one named last changes fastest.
Arguments:
- three_centre: bfloat16 [32, 4096, 384], P('aux', 'orb'), may hold values from -6 to 6
- b_screen: int32 [32, 3], P('orb'), may hold values 0 or 1
- g_occ: bfloat16 [4096, 384], P('orb'), may hold values from -0.0068359375 to 0.0068359375
- occ_screen: int32 [32, 3], P('orb'), may hold values 0 or 1
- g_vir: bfloat16 [4096, 384], P('orb'), may hold values from -0.0068359375 to 0.0068359375
- vir_screen: int32 [32, 3], P('orb'), may hold values 0 or 1
Outputs:
- response: float32 [32, 32], P('aux')
All inputs are finite; a program needn't handle non-finite values. No bound on the sum of `b_screen` or of `occ_screen` or of `vir_screen` on one device may be relied on, other than what follows from the above.
Results may differ from a plain program's by a relative error of at most 0.0029.
Values may be sent and summed in bfloat16 or wider, within the bound.
A program may use at most 128 MiB of HBM per device.

v0:
```python
import jax
import jax.numpy as jnp
from jax import lax
from jax.sharding import PartitionSpec as P


def with_halo(block, sides, width):
    for axis, dim in sides:
        count = lax.axis_size(axis)
        forward = [(i, i + 1) for i in range(count - 1)]
        backward = [(target, source) for source, target in forward]
        low = lax.ppermute(
            lax.slice_in_dim(block, block.shape[dim] - width, None, axis=dim), axis, forward
        )
        high = lax.ppermute(lax.slice_in_dim(block, 0, width, axis=dim), axis, backward)
        block = jnp.concatenate([low, block, high], axis=dim)
    return block


def tile_mask(screen, first, nob, block_size):
    count = screen.shape[0]
    blocks = (
        first
        + jnp.arange(count, dtype=jnp.int32)[:, None]
        + jnp.arange(3, dtype=jnp.int32)[None, :]
        - 1
    )
    live = (screen == 1) & (blocks >= 0) & (blocks < nob)
    return jnp.repeat(jnp.repeat(live, block_size, axis=0), block_size, axis=1)


def per_device(three_centre, b_screen, g_occ, occ_screen, g_vir, vir_screen):
    aux_dev, rows, width = three_centre.shape
    block_size = width // 3
    nbd = rows // block_size
    nob = nbd * lax.axis_size("orb")
    first = lax.axis_index("orb") * nbd
    nothing = jnp.zeros((), jnp.bfloat16)
    every_b = lax.all_to_all(three_centre, "aux", split_axis=1, concat_axis=0, tiled=True)
    b_mask = tile_mask(b_screen, first, nob, block_size)[None]
    kept_b = jnp.where(b_mask, three_centre, nothing)
    kept_o = jnp.where(tile_mask(occ_screen, first, nob, block_size), g_occ, nothing)
    kept_v = jnp.where(tile_mask(vir_screen, first, nob, block_size), g_vir, nothing)
    wide_b = with_halo(kept_b, (("orb", 1),), block_size)
    wide_v = with_halo(kept_v, (("orb", 0),), block_size)
    right = jnp.zeros((aux_dev, nbd, block_size, 5 * block_size), jnp.float32)
    for slot in range(3):
        lower = slot * block_size
        occ_slot = kept_o[:, lower : lower + block_size].reshape(nbd, block_size, block_size)
        near_b = wide_b[:, lower : lower + rows].reshape(aux_dev, nbd, block_size, width)
        term = jnp.einsum("jin,qjnk->qjik", occ_slot, near_b, preferred_element_type=jnp.float32)
        right = right.at[..., lower : lower + width].add(term)
    right_b = right.astype(jnp.bfloat16)
    parts = []
    for slot in range(3):
        lower = slot * block_size
        vir_rows = wide_v[lower : lower + rows].reshape(nbd, block_size, width)
        parts.append(
            jnp.einsum(
                "qjik,jlk->qjil",
                right_b[..., lower : lower + width],
                vir_rows,
                preferred_element_type=jnp.float32,
            )
        )
    w = jnp.concatenate(parts, axis=-1).reshape(aux_dev, rows, width)
    w = jnp.where(b_mask, w, 0.0).astype(jnp.bfloat16)
    every_w = lax.all_to_all(w, "aux", split_axis=1, concat_axis=0, tiled=True)
    partial_value = lax.dot_general(
        every_b,
        every_w,
        (((1, 2), (1, 2)), ((), ())),
        preferred_element_type=jnp.float32,
    )
    summed = lax.psum(partial_value, ("orb", "aux"))
    return lax.dynamic_slice_in_dim(summed, lax.axis_index("aux") * aux_dev, aux_dev, 0)


def solution(mesh):
    in_specs = (
        P("aux", "orb", None),
        P("orb", None),
        P("orb", None),
        P("orb", None),
        P("orb", None),
        P("orb", None),
    )
    out_specs = P("aux", None)
    return jax.shard_map(
        per_device, mesh=mesh, in_specs=in_specs, out_specs=out_specs, check_vma=False
    )
```

profile of v0, /device:TPU:0, one launch (start us, length us, event | category | flops | bytes accessed | tf_op | source)
XLA Modules:
  0.0 161.0 jit_solution(2481949846016735281)
XLA Ops:
  1.4 2.5 %broadcast_select_fusion = bf16[8,512,384]{2,1,0:T(8,128)(2,1)S(1)} fusion(bf16[8,512,384]{2,1,0:T(8,128)(2,1)} %param.12, pred[512,384]{1,0:T(8,128)(4,1)S(1)} %copy.37), kind=kLoop, calls=%fused_computation.26 | loop fusion | flops 1572864 | bytes 6488064 | tf_op jit(solution)/shard_map/jit(_where)/select_n | solution.py:41
  5.2 3.2 %collective-permute-start.1 = (bf16[8,128,384]{2,1,0:T(8,128)(2,1)}, bf16[8,128,384]{2,1,0:T(8,128)(2,1)}, u32[]{:S(2)}, u32[]{:S(2)}) collective-permute-start(bf16[8,128,384]{2,1,0:T(8,128)(2,1)} %get-tuple-element.44), channel_id=1, source_target_pairs={{0,4},{4,8},{8,12},{12,16},{16,20},{20,24},{24,28},{1,5},{5,9},{9,... | collective-permute-start | bytes 2359304 | tf_op jit(solution)/shard_map/ppermute | solution.py:12
  10.0 1.9 %copy.39 = bf16[512,384]{0,1:T(8,128)(2,1)} copy(bf16[512,384]{1,0:T(8,128)(2,1)} %param.16) | data formatting | bytes 786432 | tf_op args[4]
  13.6 5.0 %collective-permute-start = (bf16[128,384]{0,1:T(8,128)(2,1)}, bf16[128,384]{0,1:T(8,128)(2,1)}, u32[]{:S(2)}, u32[]{:S(2)}) collective-permute-start(bf16[128,384]{0,1:T(8,128)(2,1)} %get-tuple-element.47), channel_id=1, source_target_pairs={{0,4},{4,8},{8,12},{12,16},{16,20},{20,24},{24,28},{1,5},{5,9},{9,... | collective-permute-start | bytes 294920 | tf_op jit(solution)/shard_map/ppermute | solution.py:12
  19.9 5.4 %copy.57 = bf16[8,512,384]{2,0,1:T(8,128)(2,1)} copy(bf16[8,512,384]{2,1,0:T(8,128)(2,1)} %param.12) | data formatting | bytes 6291456 | tf_op args[0]
  25.4 4.7 %all-to-all-start.1 = ((bf16[8,512,384]{2,0,1:T(8,128)(2,1)}), bf16[8,512,384]{2,0,1:T(8,128)(2,1)}, u32[]{:S(2)}, u32[]{:S(2)}) async-start(bf16[8,512,384]{2,0,1:T(8,128)(2,1)} %copy.57), calls=%async_computation.1 | async-start | bytes 6291456 | tf_op jit(solution)/shard_map/all_to_all | solution.py:39
  30.2 1.9 %copy.42 = bf16[512,384]{0,1:T(8,128)(2,1)} copy(bf16[512,384]{1,0:T(8,128)(2,1)} %param.14) | data formatting | bytes 786432 | tf_op args[2]
  36.5 1.7 %copy.45 = bf16[512,128]{1,0:T(8,128)(2,1)} copy(bf16[512,128]{0,1:T(8,128)(2,1)} %get-tuple-element.50) | data formatting | bytes 262144 | tf_op jit(solution)/shard_map/slice | solution.py:49
  38.2 1.7 %copy.47 = bf16[512,128]{1,0:T(8,128)(2,1)} copy(bf16[512,128]{0,1:T(8,128)(2,1)} %get-tuple-element.49) | data formatting | bytes 262144 | tf_op jit(solution)/shard_map/slice | solution.py:49
  39.9 1.9 %pad_maximum_fusion.4 = (bf16[512,384]{0,1:T(8,128)(2,1)}, bf16[512,384]{0,1:T(8,128)(2,1)}) fusion(bf16[512,384]{0,1:T(8,128)(2,1)S(1)} %bitcast_select_fusion.2, bf16[128,384]{0,1:T(8,128)(2,1)} %collective-permute-done, bf16[128,384]{0,1:T(8,128)(2,1)} %collective-permute-done.3), kind=kLoop, calls=%fused_computation.35 | loop fusion | flops 1572864 | bytes 1376256 | tf_op jit(solution)/shard_map/concatenate | solution.py:16
  43.0 1.9 %copy.52 = bf16[512,384]{1,0:T(8,128)(2,1)} copy(bf16[512,384]{0,1:T(8,128)(2,1)} %get-tuple-element.46) | data formatting | bytes 786432 | tf_op jit(solution)/shard_map/slice | solution.py:57
  44.9 3.1 %pad_maximum_fusion.1 = (bf16[8,512,384]{2,1,0:T(8,128)(2,1)}, bf16[8,512,384]{2,1,0:T(8,128)(2,1)S(1)}) fusion(bf16[8,128,384]{2,1,0:T(8,128)(2,1)} %collective-permute-done.2, bf16[8,512,384]{2,1,0:T(8,128)(2,1)S(1)} %broadcast_select_fusion, bf16[8,128,384]{2,1,0:T(8,128)(2,1)} %collective-permute-done.1), kind=kLoop, calls=%fused_computation.13 | loop fusion | flops 12582912 | bytes 11010048 | tf_op jit(solution)/shard_map/concatenate | solution.py:16
  50.8 3.3 %fusion.2 = f32[8,4,128,640]{2,3,0,1:T(8,128)S(1)} fusion(f32[8,4,128,640]{2,3,0,1:T(8,128)S(1)} %scatter-add.10, bf16[4,128,128,1]{2,1,3,0:T(8,128)(2,1)S(1)} %bitcast.109, bf16[8,4,128,384]{3,2,1,0:T(8,128)(2,1)S(1)} %bitcast.103), kind=kOutput, calls=%fused_computation.6 | convolution fusion | flops 404226048 | bytes 15859712 | tf_op jit(solution)/shard_map/jin,qjnk->qjik/dot_general | solution.py:51
  54.1 3.3 %fusion = f32[8,4,128,640]{2,3,0,1:T(8,128)S(1)} fusion(f32[8,4,128,640]{2,3,0,1:T(8,128)S(1)} %fusion.2, bf16[4,128,128,1]{2,1,3,0:T(8,128)(2,1)S(1)} %bitcast.108, bf16[8,4,128,384]{3,2,1,0:T(8,128)(2,1)S(1)} %bitcast.105), kind=kOutput, calls=%fused_computation.1 | convolution fusion | flops 404226048 | bytes 15859712 | tf_op jit(solution)/shard_map/jin,qjnk->qjik/dot_general | solution.py:51
  57.3 3.1 %convert_element_type.6 = bf16[8,4,128,640]{2,3,0,1:T(8,128)(2,1)} convert(f32[8,4,128,640]{2,3,0,1:T(8,128)S(1)} %fusion) | non-fusion elementwise | flops 2621440 | bytes 15728640 | tf_op jit(solution)/shard_map/convert_element_type | solution.py:53
  60.5 2.8 %fusion.27 = bf16[8,4,128,128]{2,3,0,1:T(8,128)(2,1)S(1)} fusion(bf16[4,128,384,1]{2,1,3,0:T(8,128)(2,1)S(1)} %bitcast.112, bf16[8,4,128,640]{2,3,0,1:T(8,128)(2,1)} %convert_element_type.6), kind=kOutput, calls=%fused_computation.28 | convolution fusion | flops 402653184 | bytes 4587520 | tf_op jit(solution)/shard_map/qjik,jlk->qjil/dot_general | solution.py:59
  63.2 2.7 %fusion.33 = bf16[8,4,128,128]{2,3,0,1:T(8,128)(2,1)S(1)} fusion(bf16[4,128,384,1]{2,1,3,0:T(8,128)(2,1)S(1)} %bitcast.113, bf16[8,4,128,640]{2,3,0,1:T(8,128)(2,1)} %convert_element_type.6), kind=kOutput, calls=%fused_computation.30 | convolution fusion | flops 402653184 | bytes 4587520 | tf_op jit(solution)/shard_map/qjik,jlk->qjil/dot_general | solution.py:59
  67.0 2.8 %copy.54 = bf16[8,4,128,384]{3,2,1,0:T(8,128)(2,1)} copy(bf16[8,4,128,384]{2,3,0,1:T(8,128)(2,1)S(1)} %pad_maximum_fusion) | data formatting | bytes 6291456 | tf_op jit(solution)/shard_map/concatenate | solution.py:66
  69.8 2.5 %fusion.1 = bf16[8,512,384]{2,1,0:T(8,128)(2,1)S(1)} fusion(bf16[8,4,128,384]{3,2,1,0:T(8,128)(2,1)} %copy.54, pred[512,384]{1,0:T(8,128)(4,1)S(1)} %copy-done.3), kind=kLoop, calls=%fused_computation.4 | loop fusion | flops 1572864 | bytes 6488064 | tf_op jit(solution)/shard_map/convert_element_type | solution.py:67
  72.4 3.5 %copy.55 = bf16[8,512,384]{2,0,1:T(8,128)(2,1)} copy(bf16[8,512,384]{2,1,0:T(8,128)(2,1)S(1)} %fusion.1) | data formatting | bytes 6291456 | tf_op jit(solution)/shard_map/convert_element_type | solution.py:67
  75.9 4.2 %all-to-all-start = ((bf16[8,512,384]{2,0,1:T(8,128)(2,1)}), bf16[8,512,384]{2,0,1:T(8,128)(2,1)S(1)}, u32[]{:S(2)}, u32[]{:S(2)}) async-start(bf16[8,512,384]{2,0,1:T(8,128)(2,1)} %copy.55), calls=%async_computation | async-start | bytes 6291456 | tf_op jit(solution)/shard_map/all_to_all | solution.py:68
  80.0 37.2 %all-to-all-done = bf16[8,512,384]{2,0,1:T(8,128)(2,1)S(1)} async-done(((bf16[8,512,384]{2,0,1:T(8,128)(2,1)}), bf16[8,512,384]{2,0,1:T(8,128)(2,1)S(1)}, u32[]{:S(2)}, u32[]{:S(2)}) %all-to-all-start) | async-done | bytes 3145760 | tf_op jit(solution)/shard_map/all_to_all | solution.py:68
  117.3 2.8 %fusion.36 = f32[32,32]{0,1:T(8,128)S(1)} fusion(bf16[8,4,128,384]{3,0,2,1:T(8,128)(2,1)} %bitcast.34, bf16[8,4,128,384]{3,0,2,1:T(8,128)(2,1)S(1)} %bitcast.106), kind=kOutput, calls=%fused_computation.31 | convolution fusion | flops 100663296 | bytes 6295552 | tf_op jit(solution)/shard_map/dot_general | solution.py:69
  120.1 40.1 %psum.7 = f32[32,32]{0,1:T(8,128)S(1)} all-reduce(f32[32,32]{0,1:T(8,128)S(1)} %fusion.36), channel_id=1, replica_groups=mesh['orb'=8,'aux'=4] {'orb','aux'}, use_global_device_ids=true, to_apply=%region_0.1 | all-reduce | flops 1024 | bytes 8192 | tf_op jit(solution)/shard_map/psum | solution.py:75
  (52 shorter events, 17.5 us)
Async XLA Ops:
  1.4 2.5 %copy-start.2 = (pred[512,384]{1,0:T(8,128)(4,1)}, pred[512,384]{1,0:T(8,128)(4,1)S(1)}, u32[]{:S(2)}) copy-start(pred[512,384]{1,0:T(8,128)(4,1)S(1)} %copy.37) | copy-start | bytes 589828
  5.2 39.7 %collective-permute-start.1 = (bf16[8,128,384]{2,1,0:T(8,128)(2,1)}, bf16[8,128,384]{2,1,0:T(8,128)(2,1)}, u32[]{:S(2)}, u32[]{:S(2)}) collective-permute-start(bf16[8,128,384]{2,1,0:T(8,128)(2,1)} %get-tuple-element.44), channel_id=1, source_target_pairs={{0,4},{4,8},{8,12},{12,16},{16,20},{20,24},{24,28},{1,5},{5,9},{9,... | collective-permute-start | bytes 2359304 | tf_op jit(solution)/shard_map/ppermute | solution.py:12
  8.5 36.4 %collective-permute-start.2 = (bf16[8,128,384]{2,1,0:T(8,128)(2,1)}, bf16[8,128,384]{2,1,0:T(8,128)(2,1)}, u32[]{:S(2)}, u32[]{:S(2)}) collective-permute-start(bf16[8,128,384]{2,1,0:T(8,128)(2,1)} %get-tuple-element.43), channel_id=1, source_target_pairs={{4,0},{8,4},{12,8},{16,12},{20,16},{24,20},{28,24},{5,1},{9,5},{13... | collective-permute-start | bytes 2359304 | tf_op jit(solution)/shard_map/ppermute | solution.py:15
  13.6 26.2 %collective-permute-start = (bf16[128,384]{0,1:T(8,128)(2,1)}, bf16[128,384]{0,1:T(8,128)(2,1)}, u32[]{:S(2)}, u32[]{:S(2)}) collective-permute-start(bf16[128,384]{0,1:T(8,128)(2,1)} %get-tuple-element.47), channel_id=1, source_target_pairs={{0,4},{4,8},{8,12},{12,16},{16,20},{20,24},{24,28},{1,5},{5,9},{9,... | collective-permute-start | bytes 294920 | tf_op jit(solution)/shard_map/ppermute | solution.py:12
  18.6 21.2 %collective-permute-start.3 = (bf16[128,384]{0,1:T(8,128)(2,1)}, bf16[128,384]{0,1:T(8,128)(2,1)}, u32[]{:S(2)}, u32[]{:S(2)}) collective-permute-start(bf16[128,384]{0,1:T(8,128)(2,1)} %get-tuple-element.48), channel_id=1, source_target_pairs={{4,0},{8,4},{12,8},{16,12},{20,16},{24,20},{28,24},{5,1},{9,5},{13... | collective-permute-start | bytes 294920 | tf_op jit(solution)/shard_map/ppermute | solution.py:15
  25.4 50.5 %all-to-all-start.1 = ((bf16[8,512,384]{2,0,1:T(8,128)(2,1)}), bf16[8,512,384]{2,0,1:T(8,128)(2,1)}, u32[]{:S(2)}, u32[]{:S(2)}) async-start(bf16[8,512,384]{2,0,1:T(8,128)(2,1)} %copy.57), calls=%async_computation.1 | async-start | bytes 6291456 | tf_op jit(solution)/shard_map/all_to_all | solution.py:39
  44.9 3.1 %copy-start.6 = (bf16[512,128]{1,0:T(8,128)(2,1)S(1)}, bf16[512,128]{1,0:T(8,128)(2,1)}, u32[]{:S(2)}) copy-start(bf16[512,128]{1,0:T(8,128)(2,1)} %copy.43) | copy-start | bytes 393220
  49.3 1.5 copy-start.5
  50.8 3.3 %copy-start = (bf16[8,512,384]{2,1,0:T(8,128)(2,1)S(1)}, bf16[8,512,384]{2,1,0:T(8,128)(2,1)}, u32[]{:S(2)}) copy-start(bf16[8,512,384]{2,1,0:T(8,128)(2,1)} %get-tuple-element.41) | copy-start | bytes 9437188
  50.8 3.3 %copy-start.4 = (bf16[512,128]{1,0:T(8,128)(2,1)S(1)}, bf16[512,128]{1,0:T(8,128)(2,1)}, u32[]{:S(2)}) copy-start(bf16[512,128]{1,0:T(8,128)(2,1)} %copy.47) | copy-start | bytes 393220
  60.5 2.8 %copy-start.8 = (bf16[512,384]{1,0:T(8,128)(2,1)S(1)}, bf16[512,384]{1,0:T(8,128)(2,1)}, u32[]{:S(2)}) copy-start(bf16[512,384]{1,0:T(8,128)(2,1)} %copy.52) | copy-start | bytes 1179652
  60.5 5.5 %copy-start.1 = (bf16[8,4,128,640]{2,3,0,1:T(8,128)(2,1)S(1)}, bf16[8,4,128,640]{2,3,0,1:T(8,128)(2,1)}, u32[]{:S(2)}) copy-start(bf16[8,4,128,640]{2,3,0,1:T(8,128)(2,1)} %convert_element_type.6) | copy-start | bytes 15728644
  63.2 2.7 %copy-start.7 = (bf16[512,384]{1,0:T(8,128)(2,1)S(1)}, bf16[512,384]{1,0:T(8,128)(2,1)}, u32[]{:S(2)}) copy-start(bf16[512,384]{1,0:T(8,128)(2,1)} %copy.75) | copy-start | bytes 1179652
  67.0 2.8 %copy-start.3 = (pred[512,384]{1,0:T(8,128)(4,1)S(1)}, pred[512,384]{1,0:T(8,128)(4,1)}, u32[]{:S(2)}) copy-start(pred[512,384]{1,0:T(8,128)(4,1)} %copy-done.2) | copy-start | bytes 589828
  75.9 41.4 %all-to-all-start = ((bf16[8,512,384]{2,0,1:T(8,128)(2,1)}), bf16[8,512,384]{2,0,1:T(8,128)(2,1)S(1)}, u32[]{:S(2)}, u32[]{:S(2)}) async-start(bf16[8,512,384]{2,0,1:T(8,128)(2,1)} %copy.55), calls=%async_computation | async-start | bytes 6291456 | tf_op jit(solution)/shard_map/all_to_all | solution.py:68
where the time goes:
time: 162 us; the launch traced here: 161 us
  blocking collectives  40.1 us (25%)
  waiting for transfers between devices  37.3 us (23%)
  local copies, waits for them, and re-layouts  30.7 us (19%)
  starting transfers between devices  19.6 us (12%)
  matrix products  16.7 us (10%)
  other arithmetic  16.3 us (10%)
    psum x1, blocking collectives, per_device(): summed = lax.psum(partial_value, ('orb', 'aux'))  40.1 us
    all_to_all x1, waiting for transfers between devices, per_device(): every_w = lax.all_to_all(w, 'aux', split_axis=1, concat_axis=0, tiled=True)  37.2 us
    unnamed x27, local copies, waits for them, and re-layouts  9.6 us
    ppermute x2, starting transfers between devices, with_halo(): lax.ppermute(lax.slice_in_dim(block, block.shape[dim] - width, None, axis...  8.24 us
    dot_general x3, matrix products, per_device(): jnp.einsum('jin,qjnk->qjik', occ_slot, near_b, preferred_element_type=jnp...  7.75 us
    dot_general x3, matrix products, per_device(): jnp.einsum('qjik,jlk->qjil', right_b[..., lower:lower + width], vir_rows,...  6.14 us
    slice x4, local copies, waits for them, and re-layouts, per_device(): kept_o[:, lower:lower + block_size].reshape(nbd, block_size, block_size)  5.76 us
    concatenate x2, other arithmetic, with_halo(): block = jnp.concatenate([low, block, high], axis=dim)  5.03 us
  transfers between devices with their start and end apart: 6, of which 1 were waited for; matrix products, arithmetic and copies ran while one was open for 34% of the time, Pallas kernels for 0%

commit v1 on v0

v1 whole, which is shorter than its diff:
```python
import functools

import jax
import jax.numpy as jnp
from jax import lax
from jax.experimental import pallas as pl
from jax.experimental.pallas import tpu as pltpu
from jax.sharding import PartitionSpec as P

MESH = pl.DeviceIdType.MESH
TILE = 16
ORDER_LANES = 128


def xor(value, step, count):
    result = 0
    bit = 1
    while bit < count:
        result = result + lax.rem(value // bit + step // bit, 2) * bit
        bit *= 2
    return result


def kernel(
    n_orb,
    n_aux,
    b_hbm,
    o_ref,
    v_ref,
    bs_ref,
    os_ref,
    vs_ref,
    out_ref,
    kb,
    lo_b,
    hi_b,
    ko,
    kv,
    lo_v,
    hi_v,
    right,
    every_b,
    own_w,
    every_w,
    part,
    part_aux,
    part_orb,
    load_sem,
    own_sem,
    b_send,
    b_recv,
    halo_send,
    halo_recv,
    w_send,
    w_recv,
    p_send,
    p_recv,
    q_send,
    q_recv,
):
    aux_dev, rows, width = b_hbm.shape
    blk = width // 3
    nbd = rows // blk
    share = rows // n_aux
    per_block = blk // share
    naux = n_aux * aux_dev
    lanes = part.shape[-1]
    orb = lax.axis_index("orb")
    aux = lax.axis_index("aux")

    edges = [0, nbd - 1] if nbd > 1 else [0]
    inner = [j for j in range(nbd) if j not in edges]
    loads = {}
    for j in edges + inner:
        loads[j] = pltpu.make_async_copy(
            b_hbm.at[:, j * blk : (j + 1) * blk, :],
            kb.at[:, j * blk : (j + 1) * blk, :],
            load_sem.at[j],
        )
        loads[j].start()

    barrier = pltpu.get_barrier_semaphore()
    for k in range(1, n_aux):
        pl.semaphore_signal(
            barrier, inc=1, device_id=(orb, xor(aux, k, n_aux)), device_id_type=MESH
        )
    for k in range(1, n_orb):
        pl.semaphore_signal(
            barrier, inc=1, device_id=(lax.rem(orb + k, n_orb), aux), device_id_type=MESH
        )
    pl.semaphore_wait(barrier, n_aux + n_orb - 2)

    b_copies = []
    for k in range(n_aux - 1, 0, -1):
        peer = xor(aux, k, n_aux)
        copy = pltpu.make_async_remote_copy(
            src_ref=b_hbm.at[:, pl.ds(pl.multiple_of(peer * share, share), share), :],
            dst_ref=every_b.at[aux],
            send_sem=b_send.at[k],
            recv_sem=b_recv.at[k],
            device_id=(orb, peer),
            device_id_type=MESH,
        )
        copy.start()
        b_copies.append(copy)
    own_copy = pltpu.make_async_copy(
        b_hbm.at[:, pl.ds(pl.multiple_of(aux * share, share), share), :],
        every_b.at[aux],
        own_sem,
    )
    own_copy.start()

    has_low = jnp.where(orb > 0, 1, 0)
    has_high = jnp.where(orb < n_orb - 1, 1, 0)

    def factor(screen, j, t):
        value = screen[j, t]
        if j == 0 and t == 0:
            value = value * has_low
        if j == nbd - 1 and t == 2:
            value = value * has_high
        return value.astype(jnp.float32)

    def scaled(tile, scale):
        return (tile.astype(jnp.float32) * scale).astype(jnp.bfloat16)

    for j in range(nbd):
        for t in range(3):
            at = (slice(j * blk, (j + 1) * blk), slice(t * blk, (t + 1) * blk))
            kv[at] = scaled(v_ref[at], factor(vs_ref, j, t))
            ko[at] = scaled(o_ref[at], factor(os_ref, j, t))

    def screen_block(j):
        loads[j].wait()
        scales = [factor(bs_ref, j, t) for t in range(3)]

        def body(q, carry):
            for t in range(3):
                at = (q, slice(j * blk, (j + 1) * blk), slice(t * blk, (t + 1) * blk))
                kb[at] = scaled(kb[at], scales[t])
            return carry

        lax.fori_loop(0, aux_dev, body, 0)

    for j in edges:
        screen_block(j)

    def halo(index, source, target, peer):
        return pltpu.make_async_remote_copy(
            src_ref=source,
            dst_ref=target,
            send_sem=halo_send.at[index],
            recv_sem=halo_recv.at[index],
            device_id=(peer, aux),
            device_id_type=MESH,
        )

    below = lax.rem(orb + n_orb - 1, n_orb)
    above = lax.rem(orb + 1, n_orb)
    last = slice(rows - blk, rows)
    up = [
        halo(0, kv.at[last], lo_v, above),
        halo(1, kb.at[:, last, :], lo_b, above),
    ]
    down = [
        halo(2, kv.at[0:blk], hi_v, below),
        halo(3, kb.at[:, 0:blk, :], hi_b, below),
    ]

    @pl.when(orb < n_orb - 1)
    def _():
        for copy in up:
            copy.start()

    @pl.when(orb > 0)
    def _():
        for copy in down:
            copy.start()

    @pl.when(orb == 0)
    def _():
        lo_v[...] = jnp.zeros_like(lo_v)
        lo_b[...] = jnp.zeros_like(lo_b)

    @pl.when(orb == n_orb - 1)
    def _():
        hi_v[...] = jnp.zeros_like(hi_v)
        hi_b[...] = jnp.zeros_like(hi_b)

    for j in inner:
        screen_block(j)

    def near_b(j, q):
        if j < 0:
            return lo_b[q]
        if j >= nbd:
            return hi_b[q]
        return kb[q, j * blk : (j + 1) * blk, :]

    def near_v(j):
        if j < 0:
            return lo_v[...]
        if j >= nbd:
            return hi_v[...]
        return kv[j * blk : (j + 1) * blk, :]

    def w_copy(p):
        return pltpu.make_async_remote_copy(
            src_ref=own_w.at[p],
            dst_ref=every_w.at[aux],
            send_sem=w_send.at[p],
            recv_sem=w_recv.at[aux],
            device_id=(orb, p),
            device_id_type=MESH,
        )

    def one_block(j):
        def body(q, carry):
            terms = []
            for s in range(3):
                occ = ko[j * blk : (j + 1) * blk, s * blk : (s + 1) * blk]
                terms.append(
                    jnp.dot(occ, near_b(j + s - 1, q), preferred_element_type=jnp.float32)
                )
            for u in range(5):
                total = None
                for s in range(3):
                    t = u - s
                    if 0 <= t < 3:
                        piece = terms[s][:, t * blk : (t + 1) * blk]
                        total = piece if total is None else total + piece
                right[q, :, u * blk : (u + 1) * blk] = total.astype(jnp.bfloat16)
            return carry

        lax.fori_loop(0, aux_dev, body, 0)
        for s in range(3):
            rows_r = right[:, :, s * blk : s * blk + width].reshape(aux_dev * blk, width)
            value = lax.dot_general(
                rows_r,
                near_v(j + s - 1),
                (((1,), (1,)), ((), ())),
                preferred_element_type=jnp.float32,
            )
            value = (value * factor(bs_ref, j, s)).astype(jnp.bfloat16)
            value = value.reshape(aux_dev, blk, blk)
            for k in range(per_block):
                own_w[j * per_block + k, :, :, s * blk : (s + 1) * blk] = value[
                    :, k * share : (k + 1) * share
                ]
        for k in range(per_block):
            p = j * per_block + k

            @pl.when(aux != p)
            def _():
                w_copy(p).start()

    for j in inner:
        one_block(j)

    @pl.when(orb > 0)
    def _():
        for copy in up:
            copy.wait_recv()

    @pl.when(orb < n_orb - 1)
    def _():
        for copy in down:
            copy.wait_recv()

    for j in edges:
        one_block(j)

    own_copy.wait()
    for copy in b_copies:
        copy.wait_recv()

    pair_rows = lax.broadcasted_iota(jnp.int32, (naux * TILE, aux_dev * TILE), 0)
    pair_cols = lax.broadcasted_iota(jnp.int32, (naux * TILE, aux_dev * TILE), 1)
    same = (pair_rows & (TILE - 1)) == (pair_cols & (TILE - 1))
    pick_rows = lax.broadcasted_iota(jnp.int32, (aux_dev * TILE, lanes), 0) // TILE
    pick_cols = lax.broadcasted_iota(jnp.int32, (aux_dev * TILE, lanes), 1)

    def pairs(ref, source):
        total = None
        for t in range(share // TILE):
            cut = slice(t * TILE, (t + 1) * TILE)
            left = every_b[:, :, cut, :].reshape(naux * TILE, width)
            other = ref[source, :, cut, :].reshape(aux_dev * TILE, width)
            term = lax.dot_general(
                left, other, (((1,), (1,)), ((), ())), preferred_element_type=jnp.float32
            )
            total = term if total is None else total + term
        total = jnp.where(same, total, 0.0).reshape(naux, TILE, aux_dev * TILE)
        total = jnp.sum(total, axis=1)
        pick = jnp.where(pick_rows + source * aux_dev == pick_cols, 1.0, 0.0)
        value = jnp.dot(
            total, pick, precision=lax.Precision.HIGHEST, preferred_element_type=jnp.float32
        )
        return value.reshape(n_aux, aux_dev, lanes)

    part[...] = pairs(own_w, aux)
    for k in range(1, n_aux):
        source = xor(aux, k, n_aux)
        pltpu.make_async_remote_copy(
            src_ref=own_w.at[source],
            dst_ref=every_w.at[source],
            send_sem=w_send.at[source],
            recv_sem=w_recv.at[source],
            device_id=(orb, source),
            device_id_type=MESH,
        ).wait_recv()
        part[...] += pairs(every_w, source)

    p_copies = []
    for k in range(1, n_aux):
        peer = xor(aux, k, n_aux)
        copy = pltpu.make_async_remote_copy(
            src_ref=part.at[peer],
            dst_ref=part_aux.at[k],
            send_sem=p_send.at[k],
            recv_sem=p_recv.at[k],
            device_id=(orb, peer),
            device_id_type=MESH,
        )
        copy.start()
        p_copies.append(copy)
    mine = part[aux]
    for k in range(1, n_aux):
        p_copies[k - 1].wait_recv()
        mine = mine + part_aux[k]
    part_orb[orb] = mine
    q_copies = []
    for k in range(1, n_orb):
        peer = lax.rem(orb + k, n_orb)
        copy = pltpu.make_async_remote_copy(
            src_ref=part_orb.at[orb],
            dst_ref=part_orb.at[orb],
            send_sem=q_send.at[k],
            recv_sem=q_recv.at[k],
            device_id=(peer, aux),
            device_id_type=MESH,
        )
        copy.start()
        q_copies.append(copy)
    for k in range(1, n_orb):
        source = lax.rem(orb + n_orb - k, n_orb)
        pltpu.make_async_remote_copy(
            src_ref=part_orb.at[source],
            dst_ref=part_orb.at[source],
            send_sem=q_send.at[k],
            recv_sem=q_recv.at[k],
            device_id=(source, aux),
            device_id_type=MESH,
        ).wait_recv()
    result = part_orb[0]
    for k in range(1, n_orb):
        result = result + part_orb[k]
    out_ref[...] = result[:, :naux]

    for copy in b_copies + p_copies + q_copies:
        copy.wait_send()

    @pl.when(orb < n_orb - 1)
    def _():
        for copy in up:
            copy.wait_send()

    @pl.when(orb > 0)
    def _():
        for copy in down:
            copy.wait_send()

    for p in range(n_aux):

        @pl.when(aux != p)
        def _():
            w_copy(p).wait_send()


def per_device(n_orb, n_aux, three_centre, b_screen, g_occ, occ_screen, g_vir, vir_screen):
    aux_dev, rows, width = three_centre.shape
    blk = width // 3
    share = rows // n_aux
    naux = n_aux * aux_dev
    lanes = -(-naux // ORDER_LANES) * ORDER_LANES
    bf16, f32 = jnp.bfloat16, jnp.float32
    vmem = pl.BlockSpec(memory_space=pltpu.VMEM)
    smem = pl.BlockSpec(memory_space=pltpu.SMEM)
    dma = pltpu.SemaphoreType.DMA
    flops = 4 * aux_dev * rows * width * width
    return pl.pallas_call(
        functools.partial(kernel, n_orb, n_aux),
        out_shape=jax.ShapeDtypeStruct((aux_dev, naux), f32),
        in_specs=[pl.BlockSpec(memory_space=pl.ANY), vmem, vmem, smem, smem, smem],
        out_specs=vmem,
        scratch_shapes=[
            pltpu.VMEM((aux_dev, rows, width), bf16),
            pltpu.VMEM((aux_dev, blk, width), bf16),
            pltpu.VMEM((aux_dev, blk, width), bf16),
            pltpu.VMEM((rows, width), bf16),
            pltpu.VMEM((rows, width), bf16),
            pltpu.VMEM((blk, width), bf16),
            pltpu.VMEM((blk, width), bf16),
            pltpu.VMEM((aux_dev, blk, 5 * blk), bf16),
            pltpu.VMEM((n_aux, aux_dev, share, width), bf16),
            pltpu.VMEM((n_aux, aux_dev, share, width), bf16),
            pltpu.VMEM((n_aux, aux_dev, share, width), bf16),
            pltpu.VMEM((n_aux, aux_dev, lanes), f32),
            pltpu.VMEM((n_aux, aux_dev, lanes), f32),
            pltpu.VMEM((n_orb, aux_dev, lanes), f32),
            dma((rows // blk,)),
            dma,
            dma((n_aux,)),
            dma((n_aux,)),
            dma((4,)),
            dma((4,)),
            dma((n_aux,)),
            dma((n_aux,)),
            dma((n_aux,)),
            dma((n_aux,)),
            dma((n_orb,)),
            dma((n_orb,)),
        ],
        compiler_params=pltpu.CompilerParams(
            collective_id=0, has_side_effects=True, vmem_limit_bytes=56 * 1024 * 1024
        ),
        cost_estimate=pl.CostEstimate(
            flops=flops, bytes_accessed=4 * aux_dev * rows * width, transcendentals=0
        ),
    )(three_centre, g_occ, g_vir, b_screen, occ_screen, vir_screen)


def solution(mesh):
    in_specs = (
        P("aux", "orb", None),
        P("orb", None),
        P("orb", None),
        P("orb", None),
        P("orb", None),
        P("orb", None),
    )
    out_specs = P("aux", None)
    body = functools.partial(per_device, mesh.shape["orb"], mesh.shape["aux"])
    return jax.shard_map(body, mesh=mesh, in_specs=in_specs, out_specs=out_specs, check_vma=False)
```

time: 162 us -> 88.1 us (0.54)
  Pallas kernels: 0 us -> 86.6 us
  blocking collectives: 40.1 us -> 0 us
  waiting for transfers between devices: 37.3 us -> 0 us
  local copies, waits for them, and re-layouts: 30.7 us -> 1.28 us
  starting transfers between devices: 19.6 us -> 0 us
  matrix products: 16.7 us -> 0 us
  other arithmetic: 16.3 us -> 0 us
    pallas_call x0 -> x1, Pallas kernels: none -> 86.6 us  [per_device(): pl.pallas_call(functools.partial(kernel, n_orb, n_aux), out_shape=jax.Sha...]
    psum x1 -> x0, blocking collectives: 40.1 us -> none  [per_device(): summed = lax.psum(partial_value, ('orb', 'aux'))]
    all_to_all x2 -> x0, waiting for transfers between devices: 37.2 us -> none  [the longest x1 37.2 us: per_device(): every_w = lax.all_to_all(w, 'aux', split_axis=1, concat_axis=0, tiled=True)]
    dot_general x7 -> x0, matrix products: 16.7 us -> none  [the longest x3 7.75 us: per_device(): jnp.einsum('jin,qjnk->qjik', occ_slot, near_b, preferred_element_type=jnp...]
    slice x8 -> x0, local copies, waits for them, and re-layouts: 10.9 us -> none  [the longest x4 5.76 us: per_device(): kept_o[:, lower:lower + block_size].reshape(nbd, block_size, block_size)]
    ppermute x4 -> x0, starting transfers between devices: 10.8 us -> none  [the longest x2 8.24 us: with_halo(): lax.ppermute(lax.slice_in_dim(block, block.shape[dim] - width, None, axis...]
    all_to_all x2 -> x0, starting transfers between devices: 8.82 us -> none  [the longest x1 4.67 us: per_device(): lax.all_to_all(three_centre, 'aux', split_axis=1, concat_axis=0, tiled=True)]
    unnamed x27 -> x1, local copies, waits for them, and re-layouts: 9.6 us -> 1.28 us
  transfers between devices with their start and end apart: 6 -> 0, of which waited for: 1 -> 0; matrix products, arithmetic and copies ran while one was open for 34% -> 0% of each run, Pallas kernels for 0% -> 0%
where the time goes in v1:
time: 88.1 us; the launch traced here: 87.9 us
  Pallas kernels  86.6 us (98%)
  local copies, waits for them, and re-layouts  1.28 us (1%)
    pallas_call x1, Pallas kernels, per_device(): pl.pallas_call(functools.partial(kernel, n_orb, n_aux), out_shape=jax.Sha...  86.6 us

profile of v1, /device:TPU:0, one launch (start us, length us, event | category | flops | bytes accessed | tf_op | source)
XLA Modules:
  0.0 87.9 jit_solution(8492229345991207361)
XLA Ops:
  0.0 86.6 %shard_map.64 = f32[8,32]{1,0:T(8,128)} custom-call(bf16[8,512,384]{2,1,0:T(8,128)(2,1)} %b_hbm.1, bf16[512,384]{1,0:T(8,128)(2,1)} %o_ref.1, bf16[512,384]{1,0:T(8,128)(2,1)} %v_ref.1, s32[4,3]{1,0:T(4,128)} %bs_ref.1, s32[4,3]{1,0:T(4,128)} %os_ref.1, s32[4,3]{1,0:T(4,128)} %vs_ref.1), custom_call_target="tpu_custom_call" | custom-call | flops 2415919104 | bytes 6291456 | tf_op jit(solution)/shard_map/pallas_call | solution.py:391
  86.7 1.3 %copy.8 = f32[8,32]{1,0:T(8,128)} copy(f32[8,32]{1,0:T(8,128)} %shard_map.64) | data formatting | bytes 2048

commit v2 on v1

--- a/solution.py
+++ b/solution.py
@@ -25,8 +25,8 @@
     n_orb,
     n_aux,
     b_hbm,
-    o_ref,
-    v_ref,
+    o_hbm,
+    v_hbm,
     bs_ref,
     os_ref,
     vs_ref,
@@ -34,6 +34,8 @@
     kb,
     lo_b,
     hi_b,
+    o_ref,
+    v_ref,
     ko,
     kv,
     lo_v,
@@ -57,6 +59,8 @@
     p_recv,
     q_send,
     q_recv,
+    g_sem,
+    pair_acc,
 ):
     aux_dev, rows, width = b_hbm.shape
     blk = width // 3
@@ -68,6 +72,8 @@
     orb = lax.axis_index("orb")
     aux = lax.axis_index("aux")
 
+    pieces = min(4, share // TILE)
+    piece = share // pieces
     edges = [0, nbd - 1] if nbd > 1 else [0]
     inner = [j for j in range(nbd) if j not in edges]
     loads = {}
@@ -78,6 +84,11 @@
             load_sem.at[j],
         )
         loads[j].start()
+
+    v_load = pltpu.make_async_copy(v_hbm, v_ref, g_sem.at[0])
+    o_load = pltpu.make_async_copy(o_hbm, o_ref, g_sem.at[1])
+    v_load.start()
+    o_load.start()
 
     barrier = pltpu.get_barrier_semaphore()
     for k in range(1, n_aux):
@@ -124,6 +135,8 @@
     def scaled(tile, scale):
         return (tile.astype(jnp.float32) * scale).astype(jnp.bfloat16)
 
+    v_load.wait()
+    o_load.wait()
     for j in range(nbd):
         for t in range(3):
             at = (slice(j * blk, (j + 1) * blk), slice(t * blk, (t + 1) * blk))
@@ -204,12 +217,13 @@
             return hi_v[...]
         return kv[j * blk : (j + 1) * blk, :]
 
-    def w_copy(p):
+    def w_copy(p, c):
+        cut = slice(c * piece, (c + 1) * piece)
         return pltpu.make_async_remote_copy(
-            src_ref=own_w.at[p],
-            dst_ref=every_w.at[aux],
-            send_sem=w_send.at[p],
-            recv_sem=w_recv.at[aux],
+            src_ref=own_w.at[p, :, cut, :],
+            dst_ref=every_w.at[aux, :, cut, :],
+            send_sem=w_send.at[p, c],
+            recv_sem=w_recv.at[aux, c],
             device_id=(orb, p),
             device_id_type=MESH,
         )
@@ -252,7 +266,7 @@
 
             @pl.when(aux != p)
             def _():
-                w_copy(p).start()
+                w_copy(p, 0).start()
 
     for j in inner:
         one_block(j)
@@ -269,6 +283,13 @@
 
     for j in edges:
         one_block(j)
+
+    for c in range(1, pieces):
+        for p in range(n_aux):
+
+            @pl.when(aux != p)
+            def _():
+                w_copy(p, c).start()
 
     own_copy.wait()
     for copy in b_copies:
@@ -277,12 +298,10 @@
     pair_rows = lax.broadcasted_iota(jnp.int32, (naux * TILE, aux_dev * TILE), 0)
     pair_cols = lax.broadcasted_iota(jnp.int32, (naux * TILE, aux_dev * TILE), 1)
     same = (pair_rows & (TILE - 1)) == (pair_cols & (TILE - 1))
-    pick_rows = lax.broadcasted_iota(jnp.int32, (aux_dev * TILE, lanes), 0) // TILE
-    pick_cols = lax.broadcasted_iota(jnp.int32, (aux_dev * TILE, lanes), 1)
-
-    def pairs(ref, source):
+
+    def products(ref, source, begin, end):
         total = None
-        for t in range(share // TILE):
+        for t in range(begin // TILE, end // TILE):
             cut = slice(t * TILE, (t + 1) * TILE)
             left = every_b[:, :, cut, :].reshape(naux * TILE, width)
             other = ref[source, :, cut, :].reshape(aux_dev * TILE, width)
@@ -290,26 +309,42 @@
                 left, other, (((1,), (1,)), ((), ())), preferred_element_type=jnp.float32
             )
             total = term if total is None else total + term
+        return total
+
+    def diagonal(total):
         total = jnp.where(same, total, 0.0).reshape(naux, TILE, aux_dev * TILE)
-        total = jnp.sum(total, axis=1)
-        pick = jnp.where(pick_rows + source * aux_dev == pick_cols, 1.0, 0.0)
+        return jnp.sum(total, axis=1)
+
+    def placed(total, source):
+        shape = (aux_dev * TILE, lanes)
+        row = lax.broadcasted_iota(jnp.int32, shape, 0) // TILE
+        col = lax.broadcasted_iota(jnp.int32, shape, 1)
+        pick = jnp.where(row + source * aux_dev == col, 1.0, 0.0)
         value = jnp.dot(
             total, pick, precision=lax.Precision.HIGHEST, preferred_element_type=jnp.float32
         )
         return value.reshape(n_aux, aux_dev, lanes)
 
-    part[...] = pairs(own_w, aux)
-    for k in range(1, n_aux):
-        source = xor(aux, k, n_aux)
-        pltpu.make_async_remote_copy(
-            src_ref=own_w.at[source],
-            dst_ref=every_w.at[source],
-            send_sem=w_send.at[source],
-            recv_sem=w_recv.at[source],
-            device_id=(orb, source),
-            device_id_type=MESH,
-        ).wait_recv()
-        part[...] += pairs(every_w, source)
+    part[...] = placed(diagonal(products(own_w, aux, 0, share)), aux)
+    for c in range(pieces):
+        cut = slice(c * piece, (c + 1) * piece)
+        for k in range(1, n_aux):
+            source = xor(aux, k, n_aux)
+            pltpu.make_async_remote_copy(
+                src_ref=own_w.at[source, :, cut, :],
+                dst_ref=every_w.at[source, :, cut, :],
+                send_sem=w_send.at[source, c],
+                recv_sem=w_recv.at[source, c],
+                device_id=(orb, source),
+                device_id_type=MESH,
+            ).wait_recv()
+            total = products(every_w, source, c * piece, (c + 1) * piece)
+            if c > 0:
+                total = total + pair_acc[k]
+            if c < pieces - 1:
+                pair_acc[k] = total
+            else:
+                part[...] += placed(diagonal(total), source)
 
     p_copies = []
     for k in range(1, n_aux):
@@ -374,7 +409,8 @@
 
         @pl.when(aux != p)
         def _():
-            w_copy(p).wait_send()
+            for c in range(pieces):
+                w_copy(p, c).wait_send()
 
 
 def per_device(n_orb, n_aux, three_centre, b_screen, g_occ, occ_screen, g_vir, vir_screen):
@@ -382,8 +418,10 @@
     blk = width // 3
     share = rows // n_aux
     naux = n_aux * aux_dev
+    pieces = min(4, share // TILE)
     lanes = -(-naux // ORDER_LANES) * ORDER_LANES
     bf16, f32 = jnp.bfloat16, jnp.float32
+    anywhere = pl.BlockSpec(memory_space=pl.ANY)
     vmem = pl.BlockSpec(memory_space=pltpu.VMEM)
     smem = pl.BlockSpec(memory_space=pltpu.SMEM)
     dma = pltpu.SemaphoreType.DMA
@@ -391,12 +429,14 @@
     return pl.pallas_call(
         functools.partial(kernel, n_orb, n_aux),
         out_shape=jax.ShapeDtypeStruct((aux_dev, naux), f32),
-        in_specs=[pl.BlockSpec(memory_space=pl.ANY), vmem, vmem, smem, smem, smem],
+        in_specs=[anywhere, anywhere, anywhere, smem, smem, smem],
         out_specs=vmem,
         scratch_shapes=[
             pltpu.VMEM((aux_dev, rows, width), bf16),
             pltpu.VMEM((aux_dev, blk, width), bf16),
             pltpu.VMEM((aux_dev, blk, width), bf16),
+            pltpu.VMEM((rows, width), bf16),
+            pltpu.VMEM((rows, width), bf16),
             pltpu.VMEM((rows, width), bf16),
             pltpu.VMEM((rows, width), bf16),
             pltpu.VMEM((blk, width), bf16),
@@ -414,12 +454,14 @@
             dma((n_aux,)),
             dma((4,)),
             dma((4,)),
-            dma((n_aux,)),
-            dma((n_aux,)),
+            dma((n_aux, pieces)),
+            dma((n_aux, pieces)),
             dma((n_aux,)),
             dma((n_aux,)),
             dma((n_orb,)),
             dma((n_orb,)),
+            dma((2,)),
+            pltpu.VMEM((n_aux, naux * TILE, aux_dev * TILE), f32),
         ],
         compiler_params=pltpu.CompilerParams(
             collective_id=0, has_side_effects=True, vmem_limit_bytes=56 * 1024 * 1024

time: 88.1 us -> 86.3 us (0.980)
  Pallas kernels: 86.6 us -> 84.8 us
    pallas_call x1, Pallas kernels: 86.6 us -> 84.8 us  [per_device(): pl.pallas_call(functools.partial(kernel, n_orb, n_aux), out_shape=jax.Sha...]
where the time goes in v2:
time: 86.3 us; the launch traced here: 86 us
  Pallas kernels  84.8 us (98%)
  local copies, waits for them, and re-layouts  1.28 us (1%)
    pallas_call x1, Pallas kernels, per_device(): pl.pallas_call(functools.partial(kernel, n_orb, n_aux), out_shape=jax.Sha...  84.8 us

profile of v2, /device:TPU:0, one launch (start us, length us, event | category | flops | bytes accessed | tf_op | source)
XLA Modules:
  0.0 86.0 jit_solution(9571869078960562618)
XLA Ops:
  0.0 84.8 %shard_map.64 = f32[8,32]{1,0:T(8,128)} custom-call(bf16[8,512,384]{2,1,0:T(8,128)(2,1)} %b_hbm.1, bf16[512,384]{1,0:T(8,128)(2,1)} %o_hbm.1, bf16[512,384]{1,0:T(8,128)(2,1)} %v_hbm.1, s32[4,3]{1,0:T(4,128)} %bs_ref.1, s32[4,3]{1,0:T(4,128)} %os_ref.1, s32[4,3]{1,0:T(4,128)} %vs_ref.1), custom_call_target="tpu_custom_call" | custom-call | flops 2415919104 | bytes 6291456 | tf_op jit(solution)/shard_map/pallas_call | solution.py:429
  84.8 1.3 %copy.8 = f32[8,32]{1,0:T(8,128)} copy(f32[8,32]{1,0:T(8,128)} %shard_map.64) | data formatting | bytes 2048
